TPU v7x, 32 devices: a whole 2x2x4 slice. The times are simulated.
32 devices in a mesh: branch: 4 (over y, x), leaf: 8 (over z, core).
Axes of the slice: x: 2, y: 2, z: 4, core: 2. Of those that a mesh axis runs over, the one named last changes fastest.
Arguments:
- charges: bfloat16 [256, 16, 128], P(('branch', 'leaf')), may hold values from -6 to 6
- basis: bfloat16 [256, 128, 128], P(('branch', 'leaf')), may hold values from -0.5 to 0.5
- transfer0: bfloat16 [256, 128, 128], P(('branch', 'leaf')), may hold values from -0.5 to 0.5
- transfer1: bfloat16 [128, 128, 128], P(('branch', 'leaf')), may hold values from -0.5 to 0.5
- transfer2: bfloat16 [64, 128, 128], P(('branch', 'leaf')), may hold values from -0.5 to 0.5
- couple0: bfloat16 [256, 8, 128, 128], P(('branch', 'leaf')), may hold values from -0.1875 to 0.1875
- couple1: bfloat16 [128, 8, 128, 128], P(('branch', 'leaf')), may hold values from -0.1875 to 0.1875
- couple2: bfloat16 [64, 8, 128, 128], P(('branch', 'leaf')), may hold values from -0.1875 to 0.1875
- couple_top: bfloat16 [32, 8, 128, 128], P(('branch', 'leaf')), may hold values from -0.1875 to 0.1875
- list0: int32 [256, 8], P(('branch', 'leaf')), may hold values from 0 to 63, as said below
- list1: int32 [128, 8], P(('branch', 'leaf')), may hold values from 0 to 31, as said below
- list2: int32 [64, 8], P(('branch', 'leaf')), may hold values from 0 to 15, as said below
- mask0: int32 [256, 8], P(('branch', 'leaf')), may hold values from 0 to 1, as said below
- mask1: int32 [128, 8], P(('branch', 'leaf')), may hold values from 0 to 1, as said below
- mask2: int32 [64, 8], P(('branch', 'leaf')), may hold values from 0 to 1, as said below
- top_list: int32 [32, 8], P(('branch', 'leaf')), may hold values from 0 to 31
- top_mask: int32 [32, 8], P(('branch', 'leaf')), may hold values 0 or 1
- near_tiles: bfloat16 [256, 8, 128, 128], P(('branch', 'leaf')), may hold values from -0.1875 to 0.1875
- near_list: int32 [256, 8], P(('branch', 'leaf')), may hold values from 0 to 63, as said below
- near_mask: int32 [256, 8], P(('branch', 'leaf')), may hold values from 0 to 1, as said below
Outputs:
- potential: float32 [256, 16, 128], P(('branch', 'leaf'))
Inputs may be any that keep to these rules, and one draw needn't show every extreme that they name: `list0`: each entry names a leaf of the row's branch group owned by the row's device or one of the two devices beside it along leaf. `list1`: each entry names a level one cluster of the row's branch group owned by the row's device or one of the two devices beside it along leaf. `list2`: each entry names a level two cluster of the row's branch group owned by the row's device or one of the two devices beside it along leaf. `near_list`: each entry names a leaf of the row's branch group owned by the row's device or one of the two devices beside it along leaf. `mask0`: 1 marks a live entry. `mask1`: 1 marks a live entry. `mask2`: 1 marks a live entry. `near_mask`: 1 marks a live entry.
All inputs are finite; a program needn't handle non-finite values. No bound on the sum of `top_mask` on one device may be relied on, other than what follows from the above.
Results may differ from a plain program's by a relative error of at most 0.015.
Values may be sent and summed in bfloat16 or wider, within the bound.
A program may use at most 64 MiB of HBM per device.

v0:
```python
import functools

import jax
import jax.numpy as jnp
from jax import lax
from jax.experimental import pallas as pl
from jax.experimental.pallas import tpu as pltpu
from jax.sharding import PartitionSpec as P

MESH = pl.DeviceIdType.MESH
BF = jnp.bfloat16
F32 = jnp.float32


def nn(a, b):
    return lax.dot_general(a, b, (((1,), (0,)), ((), ())), preferred_element_type=F32)


def nt(a, b):
    return lax.dot_general(a, b, (((1,), (1,)), ((), ())), preferred_element_type=F32)


def gathered(table, c, wide, start, spot):
    total = None
    width = table.shape[1]
    for k in range(0, width, 2):
        left = jnp.concatenate([wide[spot(k)], wide[spot(k + 1)]], axis=1)
        right = jnp.concatenate([table[c, k], table[c, k + 1]], axis=1)
        part = nt(left, right)
        total = part if total is None else total + part
    return total


def kernel(
    n_branch,
    n_leaf,
    charges,
    basis,
    transfer0,
    transfer1,
    transfer2,
    couple0,
    couple1,
    couple2,
    couple_top,
    list0,
    list1,
    list2,
    mask0,
    mask1,
    mask2,
    top_list,
    top_mask,
    near_tiles,
    near_list,
    near_mask,
    out,
    v_basis,
    v_t0,
    v_t1,
    v_t2,
    v_c0,
    v_c1,
    v_c2,
    v_ct,
    v_near,
    s_l0,
    s_l1,
    s_l2,
    s_m0,
    s_m1,
    s_m2,
    s_tl,
    s_tm,
    s_nl,
    s_nm,
    w_ch,
    w_co,
    w_top,
    load_sem,
    list_sem,
    send_sem,
    recv_sem,
    top_send,
    top_recv,
):
    branch = lax.axis_index("branch")
    leaf = lax.axis_index("leaf")
    total = n_branch * n_leaf
    me = branch * n_leaf + leaf
    n0 = basis.shape[0]
    n1, n2 = n0 // 2, n0 // 4
    own = n0 + n1 + n2

    def around(place, step, count):
        there = place + step
        return jnp.where(there >= count, there - count, there)

    def each_device(act):
        for db in range(n_branch):
            there = around(branch, db, n_branch)
            first = 1 if db == 0 else 0
            if n_leaf <= 8:
                for dl in range(first, n_leaf):
                    act({"branch": there, "leaf": around(leaf, dl, n_leaf)})
            else:

                @pl.loop(first, n_leaf)
                def _(dl):
                    act({"branch": there, "leaf": around(leaf, dl, n_leaf)})

    loads = {}
    pairs = [
        ("ch", charges, w_ch.at[pl.ds(n0, n0)]),
        ("basis", basis, v_basis),
        ("t0", transfer0, v_t0),
        ("t1", transfer1, v_t1),
        ("t2", transfer2, v_t2),
        ("near", near_tiles, v_near),
        ("c0", couple0, v_c0),
        ("c1", couple1, v_c1),
        ("c2", couple2, v_c2),
        ("ct", couple_top, v_ct),
    ]
    for i, (name, src, dst) in enumerate(pairs):
        loads[name] = pltpu.make_async_copy(src, dst, load_sem.at[i])
    lists = []
    for i, (src, dst) in enumerate(
        [
            (near_list, s_nl),
            (near_mask, s_nm),
            (list0, s_l0),
            (mask0, s_m0),
            (list1, s_l1),
            (mask1, s_m1),
            (list2, s_l2),
            (mask2, s_m2),
            (top_list, s_tl),
            (top_mask, s_tm),
        ]
    ):
        lists.append(pltpu.make_async_copy(src, dst, list_sem.at[i]))
    for name in ("ch", "basis", "t0", "t1", "t2"):
        loads[name].start()

    barrier = pltpu.get_barrier_semaphore()

    each_device(
        lambda there: pl.semaphore_signal(barrier, inc=1, device_id=there, device_id_type=MESH)
    )

    for item in lists:
        item.start()
    for name in ("near", "c0", "c1", "c2", "ct"):
        loads[name].start()

    blank = jnp.zeros(w_ch.shape[1:], BF)
    w_ch[3 * n0] = blank
    w_co[3 * own] = blank
    w_top[total] = blank

    loads["ch"].wait()
    loads["basis"].wait()
    for c in range(n0):
        w_co[own + c] = nn(w_ch[n0 + c], v_basis[c]).astype(BF)

    def hop(buf, size, slot, step, dst_row):
        return pltpu.make_async_remote_copy(
            src_ref=buf.at[pl.ds(size, size)],
            dst_ref=buf.at[pl.ds(dst_row, size)],
            send_sem=send_sem.at[slot],
            recv_sem=recv_sem.at[slot],
            device_id={"branch": branch, "leaf": leaf + step},
            device_id_type=MESH,
        )

    ch_right = hop(w_ch, n0, 0, 1, 0)
    ch_left = hop(w_ch, n0, 1, -1, 2 * n0)
    co_right = hop(w_co, own, 2, 1, 0)
    co_left = hop(w_co, own, 3, -1, 2 * own)
    has_left = leaf > 0
    has_right = leaf < n_leaf - 1

    loads["t0"].wait()
    loads["t1"].wait()
    loads["t2"].wait()
    at = own
    for table, count in ((v_t0, n1), (v_t1, n2), (v_t2, n2 // 2)):
        for p in range(count):
            left = jnp.concatenate([w_co[at + 2 * p], w_co[at + 2 * p + 1]], axis=1)
            right = jnp.concatenate([table[2 * p], table[2 * p + 1]], axis=0)
            value = nn(left, right).astype(BF)
            if table is v_t2:
                w_top[me] = value
            else:
                w_co[at + 2 * count + p] = value
        at = at + 2 * count

    pl.semaphore_wait(barrier, total - 1)
    each_device(
        lambda there: pltpu.make_async_remote_copy(
            src_ref=w_top.at[me],
            dst_ref=w_top.at[me],
            send_sem=top_send,
            recv_sem=top_recv,
            device_id=there,
            device_id_type=MESH,
        ).start()
    )

    @pl.when(has_right)
    def _():
        ch_right.start()

    @pl.when(has_left)
    def _():
        ch_left.start()

    @pl.when(has_right)
    def _():
        co_right.start()

    @pl.when(has_left)
    def _():
        co_left.start()

    for item in lists:
        item.wait()
    loads["near"].wait()

    @pl.when(has_left)
    def _():
        ch_right.wait_recv()

    @pl.when(has_right)
    def _():
        ch_left.wait_recv()

    def where_of(links, valid, c, shift, blank_row):
        return lambda k: jnp.where(valid[c, k] != 0, links[c, k] - shift, blank_row)

    for c in range(n0):
        spot = where_of(s_nl, s_nm, c, (leaf - 1) * n0, 3 * n0)
        out[c] = gathered(v_near, c, w_ch, 0, spot)

    @pl.when(has_left)
    def _():
        co_right.wait_recv()

    @pl.when(has_right)
    def _():
        co_left.wait_recv()

    loads["c0"].wait()
    loads["c1"].wait()
    loads["c2"].wait()
    loads["ct"].wait()

    def level_spot(links, valid, c, count, start):
        def spot(k):
            j = links[c, k] - (leaf - 1) * count
            side = j // count
            row = side * own + (j - side * count) + start
            return jnp.where(valid[c, k] != 0, row, 3 * own)

        return spot

    fields = []
    for table, links, valid, count, start in (
        (v_c0, s_l0, s_m0, n0, 0),
        (v_c1, s_l1, s_m1, n1, n0),
        (v_c2, s_l2, s_m2, n2, n0 + n1),
    ):
        fields.append(
            [gathered(table, c, w_co, 0, level_spot(links, valid, c, count, start)) for c in range(count)]
        )

    everyone = w_top.at[pl.ds(0, total - 1)]
    pltpu.make_async_copy(everyone, everyone, top_recv).wait()
    local = [
        gathered(v_ct, c, w_top, 0, where_of(s_tl, s_tm, c, 0, total)).astype(BF)
        for c in range(couple_top.shape[0])
    ]
    for field, table in ((fields[2], v_t2), (fields[1], v_t1), (fields[0], v_t0)):
        below = []
        for p, parent in enumerate(local):
            both = jnp.concatenate([table[2 * p], table[2 * p + 1]], axis=0)
            spread = nt(parent, both)
            width = table.shape[1]
            below.append((field[2 * p] + spread[:, :width]).astype(BF))
            below.append((field[2 * p + 1] + spread[:, width:]).astype(BF))
        local = below
    for c in range(n0):
        out[c] += nt(local[c], v_basis[c])

    @pl.when(has_right)
    def _():
        ch_right.wait_send()
        co_right.wait_send()

    @pl.when(has_left)
    def _():
        ch_left.wait_send()
        co_left.wait_send()

    pltpu.make_async_copy(everyone, everyone, top_send).wait()


def solution(mesh):
    n_branch, n_leaf = mesh.shape["branch"], mesh.shape["leaf"]
    total = n_branch * n_leaf

    def per_device(*args):
        (charges, basis, t0, t1, t2, c0, c1, c2, ct, l0, l1, l2, m0, m1, m2, tl, tm, near, nl, nm) = args
        n0 = charges.shape[0]
        tile = charges.shape[1:]
        own = n0 + n0 // 2 + n0 // 4
        vmem = lambda x: pltpu.VMEM(x.shape, x.dtype)
        smem = lambda x: pltpu.SMEM(x.shape, x.dtype)
        dma = pltpu.SemaphoreType.DMA
        return pl.pallas_call(
            functools.partial(kernel, n_branch, n_leaf),
            out_shape=jax.ShapeDtypeStruct(charges.shape, F32),
            in_specs=[pl.BlockSpec(memory_space=pl.ANY)] * len(args),
            out_specs=pl.BlockSpec(memory_space=pltpu.VMEM),
            scratch_shapes=[
                *[vmem(x) for x in (basis, t0, t1, t2, c0, c1, c2, ct, near)],
                *[smem(x) for x in (l0, l1, l2, m0, m1, m2, tl, tm, nl, nm)],
                pltpu.VMEM((3 * n0 + 1, *tile), BF),
                pltpu.VMEM((3 * own + 1, *tile), BF),
                pltpu.VMEM((total + 1, *tile), BF),
                dma((10,)),
                dma((10,)),
                dma((4,)),
                dma((4,)),
                dma(()),
                dma(()),
            ],
            compiler_params=pltpu.CompilerParams(
                collective_id=0, has_side_effects=True, vmem_limit_bytes=63 * 1024 * 1024
            ),
        )(*args)

    three, four, two = P(("branch", "leaf"), None, None), P(("branch", "leaf"), None, None, None), P(("branch", "leaf"), None)
    return jax.shard_map(
        per_device,
        mesh=mesh,
        in_specs=(*[three] * 5, *[four] * 4, *[two] * 8, four, two, two),
        out_specs=three,
        check_vma=False,
    )
```

profile of v0, /device:TPU:1, one launch (start us, length us, event | category | flops | bytes accessed | tf_op | source)
XLA Modules:
  0.0 15.2 jit_solution(12086464640003581435)
XLA Ops:
  0.0 13.8 %shard_map.190 = f32[8,16,128]{2,1,0:T(8,128)} custom-call(bf16[8,16,128]{2,1,0:T(8,128)(2,1)} %charges.1, bf16[8,128,128]{2,1,0:T(8,128)(2,1)} %basis.1, bf16[8,128,128]{2,1,0:T(8,128)(2,1)} %transfer0.1, bf16[4,128,128]{2,1,0:T(8,128)(2,1)} %transfer1.1, bf16[2,128,128]{2,1,0:T(8,128)(2,1)} %transfer2.1, bf16[8,8,128,128]{3,2,1,0:T(8,128)(2,1)} %couple0.1, ...), custom_call_target="tpu_custom_call" | custom-call | tf_op jit(solution)/shard_map/pallas_call | solution.py:321
  13.8 1.5 %copy.22 = f32[8,16,128]{2,1,0:T(8,128)} copy(f32[8,16,128]{2,1,0:T(8,128)} %shard_map.190) | data formatting | bytes 131072
where the time goes:
time: 15.4 us; the launch traced here: 15.2 us
  Pallas kernels  13.8 us (90%)
  local copies, waits for them, and re-layouts  1.47 us (10%)
    pallas_call x1, Pallas kernels, per_device(): pl.pallas_call(functools.partial(kernel, n_branch, n_leaf), out_shape=jax...  13.8 us
    unnamed x1, local copies, waits for them, and re-layouts  1.47 us

commit v1 on v0

--- a/solution.py
+++ b/solution.py
@@ -54,7 +54,7 @@
     near_tiles,
     near_list,
     near_mask,
-    out,
+    result,
     v_basis,
     v_t0,
     v_t1,
@@ -77,6 +77,8 @@
     w_ch,
     w_co,
     w_top,
+    out,
+    out_sem,
     load_sem,
     list_sem,
     send_sem,
@@ -292,6 +294,7 @@
         local = below
     for c in range(n0):
         out[c] += nt(local[c], v_basis[c])
+        pltpu.make_async_copy(out.at[c], result.at[c], out_sem.at[c]).start()
 
     @pl.when(has_right)
     def _():
@@ -304,6 +307,8 @@
         co_left.wait_send()
 
     pltpu.make_async_copy(everyone, everyone, top_send).wait()
+    for c in range(n0):
+        pltpu.make_async_copy(out.at[c], result.at[c], out_sem.at[c]).wait()
 
 
 def solution(mesh):
@@ -322,13 +327,15 @@
             functools.partial(kernel, n_branch, n_leaf),
             out_shape=jax.ShapeDtypeStruct(charges.shape, F32),
             in_specs=[pl.BlockSpec(memory_space=pl.ANY)] * len(args),
-            out_specs=pl.BlockSpec(memory_space=pltpu.VMEM),
+            out_specs=pl.BlockSpec(memory_space=pl.ANY),
             scratch_shapes=[
                 *[vmem(x) for x in (basis, t0, t1, t2, c0, c1, c2, ct, near)],
                 *[smem(x) for x in (l0, l1, l2, m0, m1, m2, tl, tm, nl, nm)],
                 pltpu.VMEM((3 * n0 + 1, *tile), BF),
                 pltpu.VMEM((3 * own + 1, *tile), BF),
                 pltpu.VMEM((total + 1, *tile), BF),
+                pltpu.VMEM(charges.shape, F32),
+                dma((n0,)),
                 dma((10,)),
                 dma((10,)),
                 dma((4,)),

time: 15.4 us -> 15.5 us (level)
  no operation moved by 1% of the time
where the time goes in v1:
time: 15.5 us; the launch traced here: 15.4 us
  Pallas kernels  13.9 us (90%)
  local copies, waits for them, and re-layouts  1.47 us (9%)
    pallas_call x1, Pallas kernels, per_device(): pl.pallas_call(functools.partial(kernel, n_branch, n_leaf), out_shape=jax...  13.9 us
    unnamed x1, local copies, waits for them, and re-layouts  1.47 us

profile of v1, /device:TPU:1, one launch (start us, length us, event | category | flops | bytes accessed | tf_op | source)
XLA Modules:
  0.0 15.4 jit_solution(17883359826761456396)
XLA Ops:
  0.0 13.9 %shard_map.190 = f32[8,16,128]{2,1,0:T(8,128)} custom-call(bf16[8,16,128]{2,1,0:T(8,128)(2,1)} %charges.1, bf16[8,128,128]{2,1,0:T(8,128)(2,1)} %basis.1, bf16[8,128,128]{2,1,0:T(8,128)(2,1)} %transfer0.1, bf16[4,128,128]{2,1,0:T(8,128)(2,1)} %transfer1.1, bf16[2,128,128]{2,1,0:T(8,128)(2,1)} %transfer2.1, bf16[8,8,128,128]{3,2,1,0:T(8,128)(2,1)} %couple0.1, ...), custom_call_target="tpu_custom_call" | custom-call | tf_op jit(solution)/shard_map/pallas_call | solution.py:326
  13.9 1.5 %copy.22 = f32[8,16,128]{2,1,0:T(8,128)} copy(f32[8,16,128]{2,1,0:T(8,128)} %shard_map.190) | data formatting | bytes 131072
